TPU v7x, 512 devices: a whole 4x4x16 slice. The times are simulated.
512 devices in a mesh: ctx: 64 (over x_lo, z, core), tp: 8 (over x_hi, y).
Axes of the slice: x: 4 (x_hi: 2, x_lo: 2; x = x_hi * 2 + x_lo), y: 4, z: 16, core: 2. Of those that a mesh axis runs over, the one named last changes fastest.
Arguments:
- query: bfloat16 [8192, 4096], P('ctx', 'tp'), as said below
- key_proj: bfloat16 [8192, 4096], P('ctx', 'tp'), may hold values from -6 to 6
- value_proj: bfloat16 [8192, 4096], P('ctx', 'tp'), may hold values from -6 to 6
- filter_taps: bfloat16 [8192, 4096], P('ctx', 'tp'), may hold values from -6 to 6
- grad_out: bfloat16 [8192, 4096], P('ctx', 'tp'), may hold values from -6 to 6
Outputs:
- mixer_out: bfloat16 [8192, 4096], P('ctx', 'tp')
- dquery: bfloat16 [8192, 4096], P('ctx', 'tp')
- dkey: bfloat16 [8192, 4096], P('ctx', 'tp')
- dvalue: bfloat16 [8192, 4096], P('ctx', 'tp')
- dtaps: bfloat16 [8192, 4096], P('ctx', 'tp')
Inputs may be any that keep to these rules, and one draw needn't show every extreme that they name: Entries of query are real values of either sign.
All inputs are finite; a program needn't handle non-finite values.
Results may differ from a plain program's by a relative error of at most 0.0085.
Values may be sent and summed in bfloat16 or wider, within the bound.
A program may use at most 64 MiB of HBM per device.

v0:
```python
import math
import jax
import jax.numpy as jnp
from jax import lax
from jax.sharding import PartitionSpec as P

precise = lax.Precision.HIGHEST


def dft_tables(size_count):
    index = jnp.arange(size_count, dtype=jnp.int32)
    angle = (
        2.0
        * math.pi
        / size_count
        * (index[:, None] * index[None, :] % size_count).astype(jnp.float32)
    )
    return (jnp.cos(angle), jnp.sin(angle))


def twiddles(row_count, col_count):
    total = row_count * col_count
    row_index = jnp.arange(row_count, dtype=jnp.int32)
    col_index = jnp.arange(col_count, dtype=jnp.int32)
    angle = (
        2.0
        * math.pi
        / total
        * (row_index[:, None] * col_index[None, :] % total).astype(jnp.float32)
    )
    return (jnp.cos(angle), jnp.sin(angle))


def left_apply(table, blocks):
    return jnp.einsum("ka,cab->ckb", table, blocks, precision=precise)


def right_apply(blocks, table):
    return jnp.einsum("cka,ab->ckb", blocks, table, precision=precise)


def spectrum(signal):
    channels, length = signal.shape
    total = 2 * length
    row_count = 128
    col_count = total // row_count
    padded = jnp.concatenate(
        [signal.astype(jnp.float32), jnp.zeros((channels, length), jnp.float32)], axis=1
    )
    padded = padded.reshape(channels, row_count, col_count)
    cos_rows, sin_rows = dft_tables(row_count)
    cos_cols, sin_cols = dft_tables(col_count)
    cos_twist, sin_twist = twiddles(row_count, col_count)
    first_real = left_apply(cos_rows, padded)
    first_imag = -left_apply(sin_rows, padded)
    turned_real = first_real * cos_twist + first_imag * sin_twist
    turned_imag = first_imag * cos_twist - first_real * sin_twist
    spec_real = right_apply(turned_real, cos_cols) + right_apply(turned_imag, sin_cols)
    spec_imag = right_apply(turned_imag, cos_cols) - right_apply(turned_real, sin_cols)
    return (spec_real, spec_imag)


def signal_of(spec_real, spec_imag, length):
    channels, row_count, col_count = spec_real.shape
    total = row_count * col_count
    cos_rows, sin_rows = dft_tables(row_count)
    cos_cols, sin_cols = dft_tables(col_count)
    cos_twist, sin_twist = twiddles(row_count, col_count)
    back_real = right_apply(spec_real, cos_cols) - right_apply(spec_imag, sin_cols)
    back_imag = right_apply(spec_imag, cos_cols) + right_apply(spec_real, sin_cols)
    turned_real = back_real * cos_twist - back_imag * sin_twist
    turned_imag = back_imag * cos_twist + back_real * sin_twist
    values = left_apply(cos_rows, turned_real) - left_apply(sin_rows, turned_imag)
    return values.reshape(channels, total)[:, :length] / total


def times_plain(left_real, left_imag, right_real, right_imag):
    return (
        left_real * right_real - left_imag * right_imag,
        left_real * right_imag + left_imag * right_real,
    )


def times_conj(left_real, left_imag, right_real, right_imag):
    return (
        left_real * right_real + left_imag * right_imag,
        left_imag * right_real - left_real * right_imag,
    )


def channel_total(values):
    return lax.psum(values, "tp")


def per_device(query, key_proj, value_proj, filter_taps, grad_out):
    length = query.shape[0] * lax.axis_size("ctx")
    width = query.shape[1] * lax.axis_size("tp")
    filter_scale = 1.0 / math.sqrt(length)
    key_cols, value_cols, taps_cols = (
        lax.all_to_all(key_proj.T, "ctx", split_axis=0, concat_axis=1, tiled=True),
        lax.all_to_all(value_proj.T, "ctx", split_axis=0, concat_axis=1, tiled=True),
        lax.all_to_all(filter_taps.T, "ctx", split_axis=0, concat_axis=1, tiled=True),
    )
    mixed_cols = (key_cols.astype(jnp.float32) * value_cols.astype(jnp.float32)).astype(
        jnp.bfloat16
    )
    taps_real, taps_imag = spectrum(taps_cols)
    mixed_real, mixed_imag = spectrum(mixed_cols)
    conv_real, conv_imag = times_plain(mixed_real, mixed_imag, taps_real, taps_imag)
    conv_cols = (filter_scale * signal_of(conv_real, conv_imag, length)).astype(jnp.bfloat16)
    conv_rows = lax.all_to_all(conv_cols, "ctx", split_axis=1, concat_axis=0, tiled=True).T
    conv_float = conv_rows.astype(jnp.float32)
    query_float = query.astype(jnp.float32)
    gated = query_float * conv_float
    upstream = grad_out.astype(jnp.float32)
    square_sum = channel_total(jnp.sum(gated * gated, axis=1))
    inverse_rms = lax.rsqrt(square_sum / width + 1e-05)
    mixer_out = (gated * inverse_rms[:, None]).astype(jnp.bfloat16)
    dots = channel_total(jnp.sum(upstream * gated, axis=1)) / width
    dgated = inverse_rms[:, None] * upstream - (inverse_rms**3 * dots)[:, None] * gated
    dquery = (dgated * conv_float).astype(jnp.bfloat16)
    gconv = (dgated * query_float).astype(jnp.bfloat16)
    grad_cols = lax.all_to_all(gconv.T, "ctx", split_axis=0, concat_axis=1, tiled=True)
    grad_real, grad_imag = spectrum(grad_cols)
    back_real, back_imag = times_conj(grad_real, grad_imag, taps_real, taps_imag)
    dmixed_cols = (filter_scale * signal_of(back_real, back_imag, length)).astype(jnp.bfloat16)
    tap_real, tap_imag = times_conj(grad_real, grad_imag, mixed_real, mixed_imag)
    dtaps_cols = (filter_scale * signal_of(tap_real, tap_imag, length)).astype(jnp.bfloat16)
    dmixed_float = dmixed_cols.astype(jnp.float32)
    dkey_cols = (dmixed_float * value_cols.astype(jnp.float32)).astype(jnp.bfloat16)
    dvalue_cols = (dmixed_float * key_cols.astype(jnp.float32)).astype(jnp.bfloat16)
    dkey_back, dvalue_back, dtaps_back = (
        lax.all_to_all(dkey_cols, "ctx", split_axis=1, concat_axis=0, tiled=True),
        lax.all_to_all(dvalue_cols, "ctx", split_axis=1, concat_axis=0, tiled=True),
        lax.all_to_all(dtaps_cols, "ctx", split_axis=1, concat_axis=0, tiled=True),
    )
    dkey = dkey_back.T
    dvalue = dvalue_back.T
    dtaps = dtaps_back.T
    return (mixer_out, dquery, dkey, dvalue, dtaps)


def solution(mesh):
    in_specs = (P("ctx", "tp"), P("ctx", "tp"), P("ctx", "tp"), P("ctx", "tp"), P("ctx", "tp"))
    out_specs = (P("ctx", "tp"), P("ctx", "tp"), P("ctx", "tp"), P("ctx", "tp"), P("ctx", "tp"))
    return jax.shard_map(
        per_device, mesh=mesh, in_specs=in_specs, out_specs=out_specs, check_vma=False
    )
```

profile of v0, /device:TPU:1, one launch (start us, length us, event | category | flops | bytes accessed | tf_op | source)
XLA Modules:
  0.0 244.5 jit_solution(10890862937073430349)
XLA Ops:
  0.6 1.7 copy.86
  2.3 18.2 %all-to-all-start = ((bf16[64,8,128]{2,1,0:T(8,128)(2,1)}), bf16[64,8,128]{2,1,0:T(8,128)(2,1)S(1)}, u32[]{:S(2)}, u32[]{:S(2)}) async-start(bf16[64,8,128]{2,1,0:T(8,128)(2,1)} %bitcast.1), calls=%async_computation | async-start | bytes 262144 | tf_op jit(solution)/shard_map/all_to_all | solution.py:100
  20.5 0.8 copy.94
  21.3 16.4 %all-to-all-done = bf16[64,8,128]{2,1,0:T(8,128)(2,1)S(1)} async-done(((bf16[64,8,128]{2,1,0:T(8,128)(2,1)}), bf16[64,8,128]{2,1,0:T(8,128)(2,1)S(1)}, u32[]{:S(2)}, u32[]{:S(2)}) %all-to-all-start) | async-done | bytes 131104 | tf_op jit(solution)/shard_map/all_to_all | solution.py:100
  37.6 4.4 %all-to-all-start.2 = ((bf16[64,8,128]{2,1,0:T(8,128)(2,1)}), bf16[64,8,128]{2,1,0:T(8,128)(2,1)S(1)}, u32[]{:S(2)}, u32[]{:S(2)}) async-start(bf16[64,8,128]{2,1,0:T(8,128)(2,1)} %bitcast.13), calls=%async_computation.2 | async-start | bytes 262144 | tf_op jit(solution)/shard_map/all_to_all | solution.py:102
  43.4 0.8 copy.87
  44.1 15.2 %all-to-all-done.2 = bf16[64,8,128]{2,1,0:T(8,128)(2,1)S(1)} async-done(((bf16[64,8,128]{2,1,0:T(8,128)(2,1)}), bf16[64,8,128]{2,1,0:T(8,128)(2,1)S(1)}, u32[]{:S(2)}, u32[]{:S(2)}) %all-to-all-start.2) | async-done | bytes 131104 | tf_op jit(solution)/shard_map/all_to_all | solution.py:102
  59.3 4.6 %all-to-all-start.1 = ((bf16[64,8,128]{2,1,0:T(8,128)(2,1)}), bf16[64,8,128]{2,1,0:T(8,128)(2,1)S(1)}, u32[]{:S(2)}, u32[]{:S(2)}) async-start(bf16[64,8,128]{2,1,0:T(8,128)(2,1)} %bitcast.5), calls=%async_computation.1 | async-start | bytes 262144 | tf_op jit(solution)/shard_map/all_to_all | solution.py:101
  64.0 0.7 convolution_bitcast_fusion.1
  64.6 0.6 fusion.1
  65.3 15.7 %all-to-all-done.1 = bf16[64,8,128]{2,1,0:T(8,128)(2,1)S(1)} async-done(((bf16[64,8,128]{2,1,0:T(8,128)(2,1)}), bf16[64,8,128]{2,1,0:T(8,128)(2,1)S(1)}, u32[]{:S(2)}, u32[]{:S(2)}) %all-to-all-start.1) | async-done | bytes 131104 | tf_op jit(solution)/shard_map/all_to_all | solution.py:101
  81.1 0.7 convolution_bitcast_fusion.2
  81.7 0.7 fusion.2
  82.4 1.2 fusion.67
  83.6 1.2 fusion.66
  84.8 1.2 fusion.69
  86.0 1.2 fusion.68
  87.2 1.2 convolution_add_fusion.5
  88.4 1.2 convolution_subtract_fusion.7
  89.6 1.2 convolution_add_fusion.4
  90.8 1.4 multiply_subtract_fusion.3
  92.3 0.9 fusion.110
  93.1 0.9 fusion.108
  94.0 0.9 convolution_subtract_fusion.6
  94.9 0.9 convolution_add_fusion.3
  95.8 0.8 fusion.23
  96.6 0.8 fusion.5
  98.0 0.7 fusion.61
  98.7 4.6 %all-to-all-start.3 = ((bf16[8,64,128]{2,0,1:T(8,128)(2,1)}), bf16[8,64,128]{2,0,1:T(8,128)(2,1)S(1)}, u32[]{:S(2)}, u32[]{:S(2)}) async-start(bf16[8,64,128]{2,0,1:T(8,128)(2,1)} %fusion.61), calls=%async_computation.3 | async-start | bytes 262144 | tf_op jit(solution)/shard_map/all_to_all | solution.py:111
  103.4 0.8 copy-done.5
  104.3 16.2 %all-to-all-done.3 = bf16[8,64,128]{2,0,1:T(8,128)(2,1)S(1)} async-done(((bf16[8,64,128]{2,0,1:T(8,128)(2,1)}), bf16[8,64,128]{2,0,1:T(8,128)(2,1)S(1)}, u32[]{:S(2)}, u32[]{:S(2)}) %all-to-all-start.3) | async-done | bytes 131104 | tf_op jit(solution)/shard_map/all_to_all | solution.py:111
  120.6 20.4 %all-reduce.3 = (f32[128]{0:T(128)S(1)}, f32[128]{0:T(128)S(1)}) all-reduce(f32[128]{0:T(128)S(1)} %get-tuple-element.16, f32[128]{0:T(128)S(1)} %get-tuple-element.15), channel_id=1, replica_groups=mesh['ctx'=64,'tp'=8] {'tp'}, use_global_device_ids=true, to_apply=%region_1.2 | all-reduce | flops 256 | bytes 2048 | tf_op jit(solution)/shard_map/psum | solution.py:92
  140.9 0.8 fusion.65
  141.8 24.6 %all_to_all.122 = bf16[64,8,128]{2,1,0:T(8,128)(2,1)S(1)} all-to-all(bf16[64,8,128]{2,1,0:T(8,128)(2,1)S(1)} %get-tuple-element.29), channel_id=1, replica_groups=mesh['ctx'=64,'tp'=8] {'ctx'}, dimensions={0} | all-to-all | bytes 262144 | tf_op jit(solution)/shard_map/all_to_all | solution.py:123
  166.4 0.7 convolution_bitcast_fusion
  167.0 0.7 fusion
  167.7 1.2 fusion.71
  168.9 1.2 fusion.70
  170.1 1.2 convolution_add_fusion.2
  171.3 1.3 multiply_add_fusion
  172.7 0.9 fusion.97
  173.5 0.9 fusion.95
  174.4 0.9 convolution_subtract_fusion.1
  175.3 0.9 convolution_add_fusion
  176.1 0.8 fusion.9
  177.0 0.8 fusion.3
  178.5 0.7 fusion.62
  179.2 4.4 %all-to-all-start.7 = ((bf16[8,64,128]{2,0,1:T(8,128)(2,1)}), bf16[8,64,128]{2,0,1:T(8,128)(2,1)S(1)}, u32[]{:S(2)}, u32[]{:S(2)}) async-start(bf16[8,64,128]{2,0,1:T(8,128)(2,1)} %fusion.62), calls=%async_computation.7 | async-start | bytes 262144 | tf_op jit(solution)/shard_map/all_to_all | solution.py:135
  183.6 0.9 fusion.100
  184.5 0.9 fusion.102
  185.4 0.9 convolution_add_fusion.1
  186.3 0.9 convolution_subtract_fusion.3
  187.1 0.8 fusion.16
  188.0 0.8 fusion.4
  189.3 0.7 fusion.63
  190.1 10.8 %all-to-all-done.7 = bf16[8,64,128]{2,0,1:T(8,128)(2,1)S(1)} async-done(((bf16[8,64,128]{2,0,1:T(8,128)(2,1)}), bf16[8,64,128]{2,0,1:T(8,128)(2,1)S(1)}, u32[]{:S(2)}, u32[]{:S(2)}) %all-to-all-start.7) | async-done | bytes 131104 | tf_op jit(solution)/shard_map/all_to_all | solution.py:135
  200.9 20.8 %all_to_all.123 = bf16[8,64,128]{2,0,1:T(8,128)(2,1)S(1)} all-to-all(bf16[8,64,128]{2,0,1:T(8,128)(2,1)S(1)} %get-tuple-element.27), channel_id=1, replica_groups=mesh['ctx'=64,'tp'=8] {'ctx'}, dimensions={1} | all-to-all | bytes 262144 | tf_op jit(solution)/shard_map/all_to_all | solution.py:134
  221.7 4.6 %all-to-all-start.5 = ((bf16[8,64,128]{2,0,1:T(8,128)(2,1)}), bf16[8,64,128]{2,0,1:T(8,128)(2,1)S(1)}, u32[]{:S(2)}, u32[]{:S(2)}) async-start(bf16[8,64,128]{2,0,1:T(8,128)(2,1)} %get-tuple-element.28), calls=%async_computation.5 | async-start | bytes 262144 | tf_op jit(solution)/shard_map/all_to_all | solution.py:133
  226.3 0.8 copy.130
  227.2 0.8 copy.129
  228.0 0.8 copy.133
  228.8 0.8 copy.132
  229.5 14.0 %all-to-all-done.5 = bf16[8,64,128]{2,0,1:T(8,128)(2,1)S(1)} async-done(((bf16[8,64,128]{2,0,1:T(8,128)(2,1)}), bf16[8,64,128]{2,0,1:T(8,128)(2,1)S(1)}, u32[]{:S(2)}, u32[]{:S(2)}) %all-to-all-start.5) | async-done | bytes 131104 | tf_op jit(solution)/shard_map/all_to_all | solution.py:133
  243.6 0.8 copy.131
  (29 shorter events, 3.5 us)
Async XLA Ops:
  2.3 18.2 %copy-start.2 = (bf16[128,512]{1,0:T(8,128)(2,1)S(1)}, bf16[128,512]{1,0:T(8,128)(2,1)}, u32[]{:S(2)}) copy-start(bf16[128,512]{1,0:T(8,128)(2,1)} %param.8) | copy-start | bytes 393220
  2.3 35.3 %all-to-all-start = ((bf16[64,8,128]{2,1,0:T(8,128)(2,1)}), bf16[64,8,128]{2,1,0:T(8,128)(2,1)S(1)}, u32[]{:S(2)}, u32[]{:S(2)}) async-start(bf16[64,8,128]{2,1,0:T(8,128)(2,1)} %bitcast.1), calls=%async_computation | async-start | bytes 262144 | tf_op jit(solution)/shard_map/all_to_all | solution.py:100
  37.6 21.7 %all-to-all-start.2 = ((bf16[64,8,128]{2,1,0:T(8,128)(2,1)}), bf16[64,8,128]{2,1,0:T(8,128)(2,1)S(1)}, u32[]{:S(2)}, u32[]{:S(2)}) async-start(bf16[64,8,128]{2,1,0:T(8,128)(2,1)} %bitcast.13), calls=%async_computation.2 | async-start | bytes 262144 | tf_op jit(solution)/shard_map/all_to_all | solution.py:102
  42.4 0.9 copy-start.3
  59.3 21.7 %all-to-all-start.1 = ((bf16[64,8,128]{2,1,0:T(8,128)(2,1)}), bf16[64,8,128]{2,1,0:T(8,128)(2,1)S(1)}, u32[]{:S(2)}, u32[]{:S(2)}) async-start(bf16[64,8,128]{2,1,0:T(8,128)(2,1)} %bitcast.5), calls=%async_computation.1 | async-start | bytes 262144 | tf_op jit(solution)/shard_map/all_to_all | solution.py:101
  98.6 4.6 %copy-start.4 = (bf16[128,512]{1,0:T(8,128)(2,1)S(1)}, bf16[128,512]{1,0:T(8,128)(2,1)}, u32[]{:S(2)}) copy-start(bf16[128,512]{1,0:T(8,128)(2,1)} %param.5) | copy-start | bytes 393220
  98.7 21.8 %all-to-all-start.3 = ((bf16[8,64,128]{2,0,1:T(8,128)(2,1)}), bf16[8,64,128]{2,0,1:T(8,128)(2,1)S(1)}, u32[]{:S(2)}, u32[]{:S(2)}) async-start(bf16[8,64,128]{2,0,1:T(8,128)(2,1)} %fusion.61), calls=%async_computation.3 | async-start | bytes 262144 | tf_op jit(solution)/shard_map/all_to_all | solution.py:111
  103.3 0.9 copy-start.5
  179.2 21.7 %all-to-all-start.7 = ((bf16[8,64,128]{2,0,1:T(8,128)(2,1)}), bf16[8,64,128]{2,0,1:T(8,128)(2,1)S(1)}, u32[]{:S(2)}, u32[]{:S(2)}) async-start(bf16[8,64,128]{2,0,1:T(8,128)(2,1)} %fusion.62), calls=%async_computation.7 | async-start | bytes 262144 | tf_op jit(solution)/shard_map/all_to_all | solution.py:135
  221.7 4.6 %copy-start.1 = (bf16[128,512]{0,1:T(8,128)(2,1)S(1)}, bf16[128,512]{0,1:T(8,128)(2,1)}, u32[]{:S(2)}) copy-start(bf16[128,512]{0,1:T(8,128)(2,1)} %get-tuple-element.30) | copy-start | bytes 393220
  221.7 21.8 %all-to-all-start.5 = ((bf16[8,64,128]{2,0,1:T(8,128)(2,1)}), bf16[8,64,128]{2,0,1:T(8,128)(2,1)S(1)}, u32[]{:S(2)}, u32[]{:S(2)}) async-start(bf16[8,64,128]{2,0,1:T(8,128)(2,1)} %get-tuple-element.28), calls=%async_computation.5 | async-start | bytes 262144 | tf_op jit(solution)/shard_map/all_to_all | solution.py:133
  226.3 0.9 copy-start
where the time goes:
time: 248 us; the launch traced here: 245 us
  waiting for transfers between devices  88.3 us (36%)
  blocking collectives  65.8 us (27%)
  starting transfers between devices  40.9 us (16%)
  matrix products  34 us (14%)
  local copies, waits for them, and re-layouts  10.6 us (4%)
  other arithmetic  3.55 us (1%)
    dot_general x24, matrix products, right_apply(): return jnp.einsum('cka,ab->ckb', blocks, table, precision=precise)  25.1 us
    all_to_all x1, blocking collectives, per_device(): lax.all_to_all(gconv.T, 'ctx', split_axis=0, concat_axis=1, tiled=True)  24.6 us
    all_to_all x1, blocking collectives, per_device(): lax.all_to_all(dvalue_cols, 'ctx', split_axis=1, concat_axis=0, tiled=True)  20.8 us
    psum x1, blocking collectives, channel_total(): return lax.psum(values, 'tp')  20.4 us
    all_to_all x1, starting transfers between devices, per_device(): lax.all_to_all(key_proj.T, 'ctx', split_axis=0, concat_axis=1, tiled=True)  18.2 us
    all_to_all x1, waiting for transfers between devices, per_device(): lax.all_to_all(key_proj.T, 'ctx', split_axis=0, concat_axis=1, tiled=True)  16.4 us
    all_to_all x1, waiting for transfers between devices, per_device(): lax.all_to_all(conv_cols, 'ctx', split_axis=1, concat_axis=0, tiled=True)  16.2 us
    all_to_all x1, waiting for transfers between devices, per_device(): lax.all_to_all(value_proj.T, 'ctx', split_axis=0, concat_axis=1, tiled=True)  15.7 us
  transfers between devices with their start and end apart: 6, of which 6 were waited for; matrix products, arithmetic and copies ran while one was open for 5% of the time, Pallas kernels for 0%

commit v1 on v0

--- a/solution.py
+++ b/solution.py
@@ -5,6 +5,11 @@
 from jax.sharding import PartitionSpec as P
 
 precise = lax.Precision.HIGHEST
+
+
+def read_floor(load):
+    earlier = lax.all_gather(load, axis_name="tp")
+    return jnp.sum(earlier, axis=0)
 
 
 def dft_tables(size_count):
@@ -89,7 +94,7 @@
 
 
 def channel_total(values):
-    return lax.psum(values, "tp")
+    return read_floor(values)
 
 
 def per_device(query, key_proj, value_proj, filter_taps, grad_out):

time: 248 us -> 265 us (1.069)
  blocking collectives: 65.8 us -> 82.8 us
    all_gather x0 -> x2, blocking collectives: none -> 33.9 us  [read_floor(): earlier = lax.all_gather(load, axis_name='tp')]
    psum x1 -> x0, blocking collectives: 20.4 us -> none  [channel_total(): return lax.psum(values, 'tp')]
    all_to_all x1, blocking collectives: 24.6 us -> 28.1 us  [per_device(): lax.all_to_all(gconv.T, 'ctx', split_axis=0, concat_axis=1, tiled=True)]
where the time goes in v1:
time: 265 us; the launch traced here: 262 us
  waiting for transfers between devices  88.3 us (33%)
  blocking collectives  82.8 us (31%)
  starting transfers between devices  40.9 us (15%)
  matrix products  34 us (13%)
  local copies, waits for them, and re-layouts  10.6 us (4%)
  other arithmetic  3.6 us (1%)
    all_gather x2, blocking collectives, read_floor(): earlier = lax.all_gather(load, axis_name='tp')  33.9 us
    all_to_all x1, blocking collectives, per_device(): lax.all_to_all(gconv.T, 'ctx', split_axis=0, concat_axis=1, tiled=True)  28.1 us
    dot_general x24, matrix products, right_apply(): return jnp.einsum('cka,ab->ckb', blocks, table, precision=precise)  25.1 us
    all_to_all x1, blocking collectives, per_device(): lax.all_to_all(dvalue_cols, 'ctx', split_axis=1, concat_axis=0, tiled=True)  20.8 us
    all_to_all x1, starting transfers between devices, per_device(): lax.all_to_all(key_proj.T, 'ctx', split_axis=0, concat_axis=1, tiled=True)  18.2 us
    all_to_all x1, waiting for transfers between devices, per_device(): lax.all_to_all(key_proj.T, 'ctx', split_axis=0, concat_axis=1, tiled=True)  16.4 us
    all_to_all x1, waiting for transfers between devices, per_device(): lax.all_to_all(conv_cols, 'ctx', split_axis=1, concat_axis=0, tiled=True)  16.2 us
    all_to_all x1, waiting for transfers between devices, per_device(): lax.all_to_all(value_proj.T, 'ctx', split_axis=0, concat_axis=1, tiled=True)  15.7 us
  transfers between devices with their start and end apart: 6, of which 6 were waited for; matrix products, arithmetic and copies ran while one was open for 5% of the time, Pallas kernels for 0%

profile of v1, /device:TPU:1, one launch (start us, length us, event | category | flops | bytes accessed | tf_op | source)
XLA Modules:
  0.0 261.6 jit_solution(17741919336070045547)
XLA Ops:
  0.6 1.7 copy.86
  2.3 18.2 %all-to-all-start = ((bf16[64,8,128]{2,1,0:T(8,128)(2,1)}), bf16[64,8,128]{2,1,0:T(8,128)(2,1)S(1)}, u32[]{:S(2)}, u32[]{:S(2)}) async-start(bf16[64,8,128]{2,1,0:T(8,128)(2,1)} %bitcast.1), calls=%async_computation | async-start | bytes 262144 | tf_op jit(solution)/shard_map/all_to_all | solution.py:105
  20.5 0.8 copy.94
  21.3 16.4 %all-to-all-done = bf16[64,8,128]{2,1,0:T(8,128)(2,1)S(1)} async-done(((bf16[64,8,128]{2,1,0:T(8,128)(2,1)}), bf16[64,8,128]{2,1,0:T(8,128)(2,1)S(1)}, u32[]{:S(2)}, u32[]{:S(2)}) %all-to-all-start) | async-done | bytes 131104 | tf_op jit(solution)/shard_map/all_to_all | solution.py:105
  37.6 4.4 %all-to-all-start.2 = ((bf16[64,8,128]{2,1,0:T(8,128)(2,1)}), bf16[64,8,128]{2,1,0:T(8,128)(2,1)S(1)}, u32[]{:S(2)}, u32[]{:S(2)}) async-start(bf16[64,8,128]{2,1,0:T(8,128)(2,1)} %bitcast.13), calls=%async_computation.2 | async-start | bytes 262144 | tf_op jit(solution)/shard_map/all_to_all | solution.py:107
  43.4 0.8 copy.87
  44.1 15.2 %all-to-all-done.2 = bf16[64,8,128]{2,1,0:T(8,128)(2,1)S(1)} async-done(((bf16[64,8,128]{2,1,0:T(8,128)(2,1)}), bf16[64,8,128]{2,1,0:T(8,128)(2,1)S(1)}, u32[]{:S(2)}, u32[]{:S(2)}) %all-to-all-start.2) | async-done | bytes 131104 | tf_op jit(solution)/shard_map/all_to_all | solution.py:107
  59.3 4.6 %all-to-all-start.1 = ((bf16[64,8,128]{2,1,0:T(8,128)(2,1)}), bf16[64,8,128]{2,1,0:T(8,128)(2,1)S(1)}, u32[]{:S(2)}, u32[]{:S(2)}) async-start(bf16[64,8,128]{2,1,0:T(8,128)(2,1)} %bitcast.5), calls=%async_computation.1 | async-start | bytes 262144 | tf_op jit(solution)/shard_map/all_to_all | solution.py:106
  64.0 0.7 convolution_bitcast_fusion.1
  65.3 15.7 %all-to-all-done.1 = bf16[64,8,128]{2,1,0:T(8,128)(2,1)S(1)} async-done(((bf16[64,8,128]{2,1,0:T(8,128)(2,1)}), bf16[64,8,128]{2,1,0:T(8,128)(2,1)S(1)}, u32[]{:S(2)}, u32[]{:S(2)}) %all-to-all-start.1) | async-done | bytes 131104 | tf_op jit(solution)/shard_map/all_to_all | solution.py:106
  81.1 0.7 convolution_bitcast_fusion.2
  81.7 0.7 fusion.2
  82.4 1.2 fusion.67
  83.6 1.2 fusion.66
  84.8 1.2 fusion.69
  86.0 1.2 fusion.68
  87.2 1.2 convolution_add_fusion.5
  88.4 1.2 convolution_subtract_fusion.7
  89.6 1.2 convolution_add_fusion.4
  90.8 1.4 multiply_subtract_fusion.3
  92.3 0.9 fusion.110
  93.1 0.9 fusion.108
  94.0 0.9 convolution_subtract_fusion.6
  94.9 0.9 convolution_add_fusion.3
  95.8 0.8 fusion.23
  96.6 0.8 fusion.5
  98.0 0.7 fusion.61
  98.7 4.6 %all-to-all-start.3 = ((bf16[8,64,128]{2,0,1:T(8,128)(2,1)}), bf16[8,64,128]{2,0,1:T(8,128)(2,1)S(1)}, u32[]{:S(2)}, u32[]{:S(2)}) async-start(bf16[8,64,128]{2,0,1:T(8,128)(2,1)} %fusion.61), calls=%async_computation.3 | async-start | bytes 262144 | tf_op jit(solution)/shard_map/all_to_all | solution.py:116
  103.4 0.8 copy-done.5
  104.3 16.2 %all-to-all-done.3 = bf16[8,64,128]{2,0,1:T(8,128)(2,1)S(1)} async-done(((bf16[8,64,128]{2,0,1:T(8,128)(2,1)}), bf16[8,64,128]{2,0,1:T(8,128)(2,1)S(1)}, u32[]{:S(2)}, u32[]{:S(2)}) %all-to-all-start.3) | async-done | bytes 131104 | tf_op jit(solution)/shard_map/all_to_all | solution.py:116
  120.6 19.4 %all-gather.2 = f32[8,1,128]{2,1,0:T(1,128)S(1)} all-gather(f32[1,1,128]{2,1,0:T(1,128)S(1)} %bitcast.236), channel_id=2, replica_groups=mesh['ctx'=64,'tp'=8] {'tp'}, dimensions={0}, use_global_device_ids=true | all-gather | bytes 4608 | tf_op jit(solution)/shard_map/all_gather | solution.py:11
  140.0 14.5 %all-gather.3 = f32[8,1,128]{2,1,0:T(1,128)S(1)} all-gather(f32[1,1,128]{2,1,0:T(1,128)S(1)} %bitcast.235), channel_id=3, replica_groups=mesh['ctx'=64,'tp'=8] {'tp'}, dimensions={0}, use_global_device_ids=true | all-gather | bytes 4608 | tf_op jit(solution)/shard_map/all_gather | solution.py:11
  154.5 0.8 fusion.65
  155.3 28.1 %all_to_all.122 = bf16[64,8,128]{2,1,0:T(8,128)(2,1)S(1)} all-to-all(bf16[64,8,128]{2,1,0:T(8,128)(2,1)S(1)} %get-tuple-element.27), channel_id=1, replica_groups=mesh['ctx'=64,'tp'=8] {'ctx'}, dimensions={0} | all-to-all | bytes 262144 | tf_op jit(solution)/shard_map/all_to_all | solution.py:128
  183.4 0.7 convolution_bitcast_fusion
  184.1 0.7 fusion
  184.8 1.2 fusion.71
  186.0 1.2 fusion.70
  187.2 1.2 convolution_add_fusion.2
  188.4 1.3 multiply_add_fusion
  189.7 0.9 fusion.97
  190.6 0.9 fusion.95
  191.5 0.9 convolution_subtract_fusion.1
  192.3 0.9 convolution_add_fusion
  193.2 0.8 fusion.9
  194.0 0.8 fusion.3
  195.6 0.7 fusion.62
  196.3 4.5 %all-to-all-start.7 = ((bf16[8,64,128]{2,0,1:T(8,128)(2,1)}), bf16[8,64,128]{2,0,1:T(8,128)(2,1)S(1)}, u32[]{:S(2)}, u32[]{:S(2)}) async-start(bf16[8,64,128]{2,0,1:T(8,128)(2,1)} %fusion.62), calls=%async_computation.7 | async-start | bytes 262144 | tf_op jit(solution)/shard_map/all_to_all | solution.py:140
  200.7 0.9 fusion.100
  201.6 0.9 fusion.102
  202.5 0.9 convolution_add_fusion.1
  203.3 0.9 convolution_subtract_fusion.3
  204.2 0.8 fusion.16
  205.0 0.8 fusion.4
  206.4 0.7 fusion.63
  207.1 10.8 %all-to-all-done.7 = bf16[8,64,128]{2,0,1:T(8,128)(2,1)S(1)} async-done(((bf16[8,64,128]{2,0,1:T(8,128)(2,1)}), bf16[8,64,128]{2,0,1:T(8,128)(2,1)S(1)}, u32[]{:S(2)}, u32[]{:S(2)}) %all-to-all-start.7) | async-done | bytes 131104 | tf_op jit(solution)/shard_map/all_to_all | solution.py:140
  217.9 20.8 %all_to_all.123 = bf16[8,64,128]{2,0,1:T(8,128)(2,1)S(1)} all-to-all(bf16[8,64,128]{2,0,1:T(8,128)(2,1)S(1)} %get-tuple-element.25), channel_id=1, replica_groups=mesh['ctx'=64,'tp'=8] {'ctx'}, dimensions={1} | all-to-all | bytes 262144 | tf_op jit(solution)/shard_map/all_to_all | solution.py:139
  238.8 4.6 %all-to-all-start.5 = ((bf16[8,64,128]{2,0,1:T(8,128)(2,1)}), bf16[8,64,128]{2,0,1:T(8,128)(2,1)S(1)}, u32[]{:S(2)}, u32[]{:S(2)}) async-start(bf16[8,64,128]{2,0,1:T(8,128)(2,1)} %get-tuple-element.26), calls=%async_computation.5 | async-start | bytes 262144 | tf_op jit(solution)/shard_map/all_to_all | solution.py:138
  243.4 0.8 copy.130
  244.3 0.8 copy.129
  245.1 0.8 copy.133
  245.8 0.8 copy.132
  246.6 14.0 %all-to-all-done.5 = bf16[8,64,128]{2,0,1:T(8,128)(2,1)S(1)} async-done(((bf16[8,64,128]{2,0,1:T(8,128)(2,1)}), bf16[8,64,128]{2,0,1:T(8,128)(2,1)S(1)}, u32[]{:S(2)}, u32[]{:S(2)}) %all-to-all-start.5) | async-done | bytes 131104 | tf_op jit(solution)/shard_map/all_to_all | solution.py:138
  260.6 0.8 copy.131
  (32 shorter events, 4.2 us)
Async XLA Ops:
  2.3 18.2 %copy-start.2 = (bf16[128,512]{1,0:T(8,128)(2,1)S(1)}, bf16[128,512]{1,0:T(8,128)(2,1)}, u32[]{:S(2)}) copy-start(bf16[128,512]{1,0:T(8,128)(2,1)} %param.8) | copy-start | bytes 393220
  2.3 35.3 %all-to-all-start = ((bf16[64,8,128]{2,1,0:T(8,128)(2,1)}), bf16[64,8,128]{2,1,0:T(8,128)(2,1)S(1)}, u32[]{:S(2)}, u32[]{:S(2)}) async-start(bf16[64,8,128]{2,1,0:T(8,128)(2,1)} %bitcast.1), calls=%async_computation | async-start | bytes 262144 | tf_op jit(solution)/shard_map/all_to_all | solution.py:105
  37.6 21.7 %all-to-all-start.2 = ((bf16[64,8,128]{2,1,0:T(8,128)(2,1)}), bf16[64,8,128]{2,1,0:T(8,128)(2,1)S(1)}, u32[]{:S(2)}, u32[]{:S(2)}) async-start(bf16[64,8,128]{2,1,0:T(8,128)(2,1)} %bitcast.13), calls=%async_computation.2 | async-start | bytes 262144 | tf_op jit(solution)/shard_map/all_to_all | solution.py:107
  42.4 0.9 copy-start.3
  59.3 21.7 %all-to-all-start.1 = ((bf16[64,8,128]{2,1,0:T(8,128)(2,1)}), bf16[64,8,128]{2,1,0:T(8,128)(2,1)S(1)}, u32[]{:S(2)}, u32[]{:S(2)}) async-start(bf16[64,8,128]{2,1,0:T(8,128)(2,1)} %bitcast.5), calls=%async_computation.1 | async-start | bytes 262144 | tf_op jit(solution)/shard_map/all_to_all | solution.py:106
  98.6 4.6 %copy-start.4 = (bf16[128,512]{1,0:T(8,128)(2,1)S(1)}, bf16[128,512]{1,0:T(8,128)(2,1)}, u32[]{:S(2)}) copy-start(bf16[128,512]{1,0:T(8,128)(2,1)} %param.5) | copy-start | bytes 393220
  98.7 21.8 %all-to-all-start.3 = ((bf16[8,64,128]{2,0,1:T(8,128)(2,1)}), bf16[8,64,128]{2,0,1:T(8,128)(2,1)S(1)}, u32[]{:S(2)}, u32[]{:S(2)}) async-start(bf16[8,64,128]{2,0,1:T(8,128)(2,1)} %fusion.61), calls=%async_computation.3 | async-start | bytes 262144 | tf_op jit(solution)/shard_map/all_to_all | solution.py:116
  103.3 0.9 copy-start.5
  196.3 21.7 %all-to-all-start.7 = ((bf16[8,64,128]{2,0,1:T(8,128)(2,1)}), bf16[8,64,128]{2,0,1:T(8,128)(2,1)S(1)}, u32[]{:S(2)}, u32[]{:S(2)}) async-start(bf16[8,64,128]{2,0,1:T(8,128)(2,1)} %fusion.62), calls=%async_computation.7 | async-start | bytes 262144 | tf_op jit(solution)/shard_map/all_to_all | solution.py:140
  238.8 4.6 %copy-start.1 = (bf16[128,512]{0,1:T(8,128)(2,1)S(1)}, bf16[128,512]{0,1:T(8,128)(2,1)}, u32[]{:S(2)}) copy-start(bf16[128,512]{0,1:T(8,128)(2,1)} %get-tuple-element.28) | copy-start | bytes 393220
  238.8 21.8 %all-to-all-start.5 = ((bf16[8,64,128]{2,0,1:T(8,128)(2,1)}), bf16[8,64,128]{2,0,1:T(8,128)(2,1)S(1)}, u32[]{:S(2)}, u32[]{:S(2)}) async-start(bf16[8,64,128]{2,0,1:T(8,128)(2,1)} %get-tuple-element.26), calls=%async_computation.5 | async-start | bytes 262144 | tf_op jit(solution)/shard_map/all_to_all | solution.py:138
  243.4 0.9 copy-start
